TPU v7x, 32 devices: a whole 2x2x4 slice. The times are simulated.
32 devices in a mesh: req: 8 (over y, x, core), tp: 4 (over z).
Axes of the slice: x: 2, y: 2, z: 4, core: 2. Of those that a mesh axis runs over, the one named last changes fastest.
Arguments:
- activations: bfloat16 [2048, 2304], P('req'), may hold values from -6 to 6
- lengths: int32 [8, 4], P('req'), may hold values from 1 to 192, 256 in all within a row
- adapter_of: int32 [8, 4], P('req'), may hold values from 0 to 15
- slot_of: int32 [16], replicated, may hold values from 0 to 15, as said below
- page_table: int32 [8, 6], P('req'), may hold values from 0 to 5, each once within a row
- experts_of: int32 [2048, 2], P('req'), may hold values from 0 to 7, all different within a row; in each aligned block of 256 rows (0 to 255, 256 to 511, ...) at most 72 rows name the same one
- attn_gain: float32 [2304], replicated, may hold values from 0.25 to 1.75
- moe_gain: float32 [2304], replicated, may hold values from 0.25 to 1.75
- w_qkv: bfloat16 [2304, 3, 2304], P(None, None, 'tp'), may hold values from -4 to 4
- output_weight: bfloat16 [2304, 2304], P('tp'), may hold values from -0.125 to 0.125
- router: bfloat16 [2304, 8], replicated, may hold values from -0.125 to 0.125
- w_gate_up: bfloat16 [8, 2304, 2, 5760], P('req', None, None, 'tp'), may hold values from -0.125 to 0.125
- w_down: bfloat16 [8, 5760, 2304], P('req', 'tp'), may hold values from -0.078125 to 0.078125
- expert_up_factors: bfloat16 [8, 256, 2, 5760], P('req', None, None, 'tp'), may hold values from -0.59765625 to 0.59765625
- pool_a: bfloat16 [16, 2304, 64], P('req'), may hold values from -0.125 to 0.125
- slot_query_key_value_up: bfloat16 [16, 16, 3, 2304], P('req', None, None, 'tp'), may hold values from -0.59765625 to 0.59765625
- pool_aout: bfloat16 [16, 2304, 16], P('req', 'tp'), may hold values from -0.125 to 0.125
- pool_bout: bfloat16 [16, 16, 2304], P('req'), may hold values from -1.796875 to 1.796875
Outputs:
- layer_out: bfloat16 [2048, 2304], P('req')
- page_cache: bfloat16 [48, 128, 2, 2304], P('req', None, None, 'tp')
Inputs may be any that keep to these rules, and one draw needn't show every extreme that they name: `slot_of`: distinct slots. `page_table`: each row holds every page index once. `experts_of`: the two experts of a token differ; among the 256 tokens of one index of req at most 72 choose one expert, and some expert reaches 72.
All inputs are finite; a program needn't handle non-finite values.
Results may differ from a plain program's by a relative error of at most 0.0095.
Values may be sent and summed in bfloat16 or wider, within the bound.
A program may use at most 128 MiB of HBM per device.

v0:
```python
import math
import jax
import jax.numpy as jnp
from jax import lax
from jax.sharding import PartitionSpec as P

D = 2304
HEAD_SIZE = 64
EXPERTS = 8
ADAPTER_RANK = 16
ADAPTER_TOTAL = 16
PAGE = 128
CAP = 72
epsilon = 1e-05
adapter_scale = 2.0
rope_base = 10000.0


def rms_norm(values, scales):
    mean_sq = jnp.mean(values * values, axis=-1, keepdims=True)
    return values * lax.rsqrt(mean_sq + epsilon) * scales


def token_layout(lengths_row, tok_count):
    ends_at = jnp.cumsum(lengths_row)
    starts = ends_at - lengths_row
    places = jnp.arange(tok_count, dtype=jnp.int32)
    request = jnp.sum((places[:, None] >= ends_at[None, :]).astype(jnp.int32), axis=1)
    position = places - starts[request]
    return (request, position)


def rotate(values, position):
    head_dim = values.shape[-1]
    half_dim = head_dim // 2
    frequency = rope_base ** (-jnp.arange(half_dim, dtype=jnp.float32) * 2.0 / head_dim)
    angles = position.astype(jnp.float32)[:, None] * frequency[None, :]
    cosine = jnp.cos(angles)[:, None, :]
    sine_part = jnp.sin(angles)[:, None, :]
    front_half = values[..., :half_dim]
    back_half = values[..., half_dim:]
    return jnp.concatenate(
        [front_half * cosine - back_half * sine_part, back_half * cosine + front_half * sine_part],
        axis=-1,
    )


def per_device(
    activations,
    lengths,
    adapter_of,
    slot_of,
    page_table,
    experts_of,
    attn_gain,
    moe_gain,
    w_qkv,
    output_weight,
    router,
    w_gate_up,
    w_down,
    expert_up_factors,
    pool_a,
    slot_query_key_value_up,
    pool_aout,
    pool_bout,
):
    token_share = activations.shape[0]
    n_req = lax.axis_size("req")
    request, position = token_layout(lengths[0], token_share)
    adapter = adapter_of[0][request]
    token_slot = slot_of[adapter]
    pool_down, slot_up_factors, pool_head, pool_outup = (
        lax.all_gather(pool_a, "req", axis=0, tiled=True),
        lax.all_gather(slot_query_key_value_up, "req", axis=0, tiled=True),
        lax.all_gather(pool_aout, "req", axis=0, tiled=True),
        lax.all_gather(pool_bout, "req", axis=0, tiled=True),
    )
    slot_count = pool_down.shape[0]
    slot_hot = token_slot[:, None] == jnp.arange(slot_count, dtype=jnp.int32)[None, :]
    head_width = w_qkv.shape[2]
    heads_number = head_width // HEAD_SIZE
    normed = rms_norm(activations.astype(jnp.float32), attn_gain).astype(jnp.bfloat16)
    down_all = jnp.einsum(
        "td,sdr->tsr",
        normed,
        pool_down[:, :, : 3 * ADAPTER_RANK],
        preferred_element_type=jnp.float32,
    )
    coeff_qkv = jnp.sum(jnp.where(slot_hot[:, :, None], down_all, 0.0), axis=1).astype(jnp.bfloat16)
    spread_rows = jnp.where(
        slot_hot[:, :, None, None],
        coeff_qkv.reshape(token_share, 1, 3, ADAPTER_RANK),
        jnp.zeros((), jnp.bfloat16),
    )
    adapter_query_key_value = jnp.einsum(
        "qwxv,wvxd->qxd", spread_rows, slot_up_factors, preferred_element_type=jnp.float32
    )
    plain_query_key_value = jnp.dot(
        normed, w_qkv.reshape(D, 3 * head_width), preferred_element_type=jnp.float32
    ).reshape(token_share, 3, head_width)
    projection_result = (plain_query_key_value + adapter_scale * adapter_query_key_value).reshape(
        token_share, 3, heads_number, HEAD_SIZE
    )
    queries = rotate(projection_result[:, 0], position).astype(jnp.bfloat16)
    keys_roped = rotate(projection_result[:, 1], position).astype(jnp.bfloat16)
    values = projection_result[:, 2].astype(jnp.bfloat16)
    pool_dev = page_table.shape[1]
    pages_used = (lengths[0] + PAGE - 1) // PAGE
    first_page = jnp.cumsum(pages_used) - pages_used
    local_page = page_table[0][first_page[request] + position // PAGE]
    cache_row = local_page * PAGE + position % PAGE
    place_hot = (
        jnp.arange(pool_dev * PAGE, dtype=jnp.int32)[:, None] == cache_row[None, :]
    ).astype(jnp.bfloat16)
    key_value = jnp.stack(
        [keys_roped.reshape(token_share, head_width), values.reshape(token_share, head_width)],
        axis=1,
    ).reshape(token_share, 2 * head_width)
    page_cache = (
        jnp.dot(place_hot, key_value, preferred_element_type=jnp.float32)
        .astype(jnp.bfloat16)
        .reshape(pool_dev, PAGE, 2, head_width)
    )
    scores = jnp.einsum("qhd,khd->hqk", queries, keys_roped, preferred_element_type=jnp.float32) * (
        1.0 / math.sqrt(HEAD_SIZE)
    )
    allowed = (request[:, None] == request[None, :]) & (position[None, :] <= position[:, None])
    scores = jnp.where(allowed[None], scores, -1e30)
    row_max = jnp.max(scores, axis=-1, keepdims=True)
    weights = jnp.exp(scores - row_max)
    weights = (weights / jnp.sum(weights, axis=-1, keepdims=True)).astype(jnp.bfloat16)
    attention_result = (
        jnp.einsum("hqk,khd->qhd", weights, values, preferred_element_type=jnp.float32)
        .astype(jnp.bfloat16)
        .reshape(token_share, head_width)
    )
    aout_all = jnp.einsum(
        "tc,scr->tsr", attention_result, pool_head, preferred_element_type=jnp.float32
    )
    coeff_out = jnp.sum(jnp.where(slot_hot[:, :, None], aout_all, 0.0), axis=1)
    spread_out = jnp.where(slot_hot[:, :, None], coeff_out[:, None, :], 0.0).reshape(
        token_share, slot_count * ADAPTER_RANK
    )
    output_update = jnp.dot(
        spread_out,
        pool_outup.astype(jnp.float32).reshape(slot_count * ADAPTER_RANK, D),
        precision=lax.Precision.HIGHEST,
    )
    head_term = (
        jnp.dot(attention_result, output_weight, preferred_element_type=jnp.float32)
        + adapter_scale * output_update
    )
    mixed_out = lax.psum(head_term, "tp")
    residual_stream = activations.astype(jnp.float32) + mixed_out
    normed_moe = rms_norm(residual_stream, moe_gain).astype(jnp.bfloat16)
    logits = jnp.dot(normed_moe, router, preferred_element_type=jnp.float32)
    chosen = jnp.take_along_axis(logits, experts_of, axis=1)
    gate_weights = 1.0 / (1.0 + jnp.exp(chosen[:, ::-1] - chosen))
    exp_all = jnp.einsum(
        "td,sdr->tsr",
        normed_moe,
        pool_down[:, :, 3 * ADAPTER_RANK :],
        preferred_element_type=jnp.float32,
    )
    coeff_exp = jnp.sum(jnp.where(slot_hot[:, :, None], exp_all, 0.0), axis=1).astype(jnp.bfloat16)
    capacity = CAP
    split_count = n_req // EXPERTS
    flat_expert = experts_of.reshape(-1)
    expert_hot = (flat_expert[:, None] == jnp.arange(EXPERTS, dtype=jnp.int32)[None, :]).astype(
        jnp.int32
    )
    order_in = jnp.sum((jnp.cumsum(expert_hot, axis=0) - expert_hot) * expert_hot, axis=1)
    column = flat_expert * capacity + order_in
    pick = (column[:, None] == jnp.arange(EXPERTS * capacity, dtype=jnp.int32)[None, :]).reshape(
        token_share, 2, EXPERTS * capacity
    )
    route = jnp.any(pick, axis=1).astype(jnp.bfloat16)
    combine_weights = jnp.sum(jnp.where(pick, gate_weights[:, :, None], 0.0), axis=1)

    def spread_copies(array):
        shaped = array.reshape((EXPERTS, 1, capacity) + array.shape[1:])
        return jnp.broadcast_to(shaped, (EXPERTS, split_count, capacity) + array.shape[1:]).reshape(
            (n_req, capacity) + array.shape[1:]
        )

    send_coeff = jnp.einsum(
        "ts,tr->sr", route, coeff_exp, preferred_element_type=jnp.float32
    ).astype(jnp.bfloat16)
    send_ids = jnp.einsum(
        "ts,t->s", route, adapter.astype(jnp.bfloat16), preferred_element_type=jnp.float32
    ).astype(jnp.bfloat16)
    adapter_range = jnp.arange(ADAPTER_TOTAL, dtype=jnp.int32).astype(jnp.bfloat16)
    send_rows = jnp.einsum(
        "ts,td->sd", route, normed_moe, preferred_element_type=jnp.float32
    ).astype(jnp.bfloat16)
    expert_input_rows = lax.all_to_all(
        spread_copies(send_rows), "req", split_axis=0, concat_axis=0, tiled=True
    )
    coeff_rank = lax.all_to_all(
        spread_copies(send_coeff), "req", split_axis=0, concat_axis=0, tiled=True
    )
    adapter_ids = lax.all_to_all(
        spread_copies(send_ids), "req", split_axis=0, concat_axis=0, tiled=True
    )
    count = expert_input_rows.shape[1]
    flat_rows = expert_input_rows.reshape(n_req * count, D)
    flat_coeff = coeff_rank.reshape(n_req * count, ADAPTER_RANK)
    flat_ids = adapter_ids.reshape(n_req * count)
    unit_count = w_gate_up.shape[3]
    broad_coefficients = jnp.where(
        flat_ids[:, None, None] == adapter_range[None, :, None],
        flat_coeff[:, None, :],
        jnp.zeros((), jnp.bfloat16),
    ).reshape(n_req * count, ADAPTER_TOTAL * ADAPTER_RANK)
    before_norm = jnp.dot(
        flat_rows, w_gate_up[0].reshape(D, 2 * unit_count), preferred_element_type=jnp.float32
    )
    before_norm = before_norm + adapter_scale * jnp.dot(
        broad_coefficients,
        expert_up_factors[0].reshape(ADAPTER_TOTAL * ADAPTER_RANK, 2 * unit_count),
        preferred_element_type=jnp.float32,
    )
    hidden = (jax.nn.silu(before_norm[:, :unit_count]) * before_norm[:, unit_count:]).astype(
        jnp.bfloat16
    )
    partial_term = jnp.dot(hidden, w_down[0], preferred_element_type=jnp.float32).astype(
        jnp.bfloat16
    )
    returned = lax.all_to_all(
        partial_term.reshape(n_req, count, D), "req", split_axis=0, concat_axis=0, tiled=True
    )
    summed = jnp.sum(
        returned.astype(jnp.float32).reshape(EXPERTS, split_count, capacity, D), axis=1
    ).reshape(EXPERTS * capacity, D)
    moe_part = jnp.dot(combine_weights, summed, precision=lax.Precision.HIGHEST)
    moe_sum = lax.psum(moe_part.astype(jnp.bfloat16), "tp").astype(jnp.float32)
    layer_out = (residual_stream + moe_sum).astype(jnp.bfloat16)
    return (layer_out, page_cache)


def solution(mesh):
    return jax.shard_map(
        per_device,
        mesh=mesh,
        in_specs=(
            P("req", None),
            P("req", None),
            P("req", None),
            P(),
            P("req", None),
            P("req", None),
            P(),
            P(),
            P(None, None, "tp"),
            P("tp", None),
            P(),
            P("req", None, None, "tp"),
            P("req", "tp", None),
            P("req", None, None, "tp"),
            P("req", None, None),
            P("req", None, None, "tp"),
            P("req", "tp", None),
            P("req", None, None),
        ),
        out_specs=(P("req", None), P("req", None, None, "tp")),
        check_vma=False,
    )
```

profile of v0, /device:TPU:0, one launch (start us, length us, event | category | flops | bytes accessed | tf_op | source)
XLA Modules:
  0.0 364.0 jit_solution(4491412793175182737)
XLA Ops:
  7.2 0.7 all-gather.3.cloned.1.call-update
  8.0 0.7 all-gather.5.cloned.1.call-update
  8.7 0.7 and_select_fusion.4
  9.4 0.8 reduce-window.27
  10.4 0.8 bitcast_subtract_fusion.2
  11.3 1.6 fusion.10
  12.9 1.5 fusion.63
  14.3 1.5 fusion.66
  15.8 2.0 fusion.62
  17.8 6.8 %compare_select_fusion.9 = (s32[256,1]{0,1:T(1,128)S(1)}, s32[256,1]{0,1:T(1,128)S(1)}, s32[256,1]{0,1:T(1,128)S(1)}) fusion(s32[]{:T(128)} %bitcast.20, s32[]{:T(128)} %bitcast.21, s32[]{:T(128)} %bitcast.22, s32[]{:T(128)} %bitcast.23, s32[]{:T(128)} %bitcast.24, s32[]{:T(128)} %bitcast.26, s32[]{:T(128)} %bitcast.25, s32[]{:T(128)} %bitcast.10, ...), kind=kLoop, calls=%fused_computation.105 | loop fusion | flops 6144 | bytes 4140 | tf_op jit(solution)/shard_map/gather | solution.py:72
  24.6 5.7 %select_select_fusion.2 = s32[256]{0:T(256)S(1)} fusion(pred[256]{0:T(512)(128)(4,1)S(1)} %get-tuple-element.22, pred[256]{0:T(512)(128)(4,1)S(1)} %get-tuple-element.21, pred[256]{0:T(512)(128)(4,1)S(1)} %get-tuple-element.20, pred[256]{0:T(512)(128)(4,1)S(1)} %get-tuple-element.19, pred[256]{0:T(512)(128)(4,1)S(1)} %get-tuple-element.18, ...), kind=kLoop, calls=%fused_computation.137 | loop fusion | flops 2304 | bytes 4388 | tf_op jit(solution)/shard_map/gather | solution.py:72
  30.3 0.7 fusion.64
  31.0 8.8 %fusion.49 = (s32[256,1]{0,1:T(1,128)S(1)}, s32[256,1]{0,1:T(1,128)S(1)}) fusion(s32[]{:T(128)} %bitcast.71, s32[]{:T(128)} %bitcast.72, s32[]{:T(128)} %bitcast.73, s32[]{:T(128)} %bitcast.67, s32[]{:T(128)} %bitcast.74, s32[]{:T(128)} %bitcast.68, s32[]{:T(128)} %bitcast.76, s32[]{:T(128)} %bitcast.75, s32[]{:T(128)} %bitcast.70, s32[]{:T(128)} %bitcast.69, ...), kind=kLoop, calls=%fused_computation.132 | loop fusion | flops 11008 | bytes 3128 | tf_op jit(solution)/shard_map/mul | solution.py:112
  40.0 12.0 %all_gather.14 = bf16[16,576,16]{1,2,0:T(8,128)(2,1)S(1)} all-gather(bf16[2,576,16]{1,2,0:T(8,128)(2,1)} %param.34), channel_id=1, replica_groups=mesh['req'=8,'tp'=4] {'req'}, dimensions={0}, use_global_device_ids=true | all-gather | bytes 331776 | tf_op jit(solution)/shard_map/all_gather | solution.py:76
  52.0 12.0 %all_gather.13 = bf16[16,16,3,576]{3,1,2,0:T(8,128)(2,1)} all-gather(bf16[2,16,3,576]{3,1,2,0:T(8,128)(2,1)S(1)} %copy-done.14), channel_id=1, replica_groups=mesh['req'=8,'tp'=4] {'req'}, dimensions={0}, use_global_device_ids=true | all-gather | bytes 995328 | tf_op jit(solution)/shard_map/all_gather | solution.py:75
  64.0 0.2 multiply_cosine_fusion
  64.2 6.8 %fusion.1 = f32[256,3,576]{0,2,1:T(8,128)} fusion(bf16[2304,3,576]{0,2,1:T(8,128)(2,1)} %param.26, bf16[256,2304]{1,0:T(8,128)(2,1)S(1)} %copy-done.5, f32[2304]{0:T(1024)S(1)} %copy-done.18, f32[256]{0:T(256)S(1)} %add_rsqrt_fusion.1), kind=kOutput, calls=%fused_computation.2 | convolution fusion | flops 2040791040 | bytes 10921984 | tf_op jit(solution)/shard_map/dot_general | solution.py:99
  71.0 1.5 copy-done.6
  72.5 1.1 slice-done
  73.6 1.2 fusion.25
  74.9 0.5 copy-done.10
  75.4 0.5 bitcast_add_fusion
  75.9 1.2 copy-done.8
  77.2 0.8 subtract_convert_fusion
  78.1 3.4 fusion.67
  81.5 2.2 convolution_convert_fusion.3
  83.7 0.3 fusion.74
  84.1 2.5 fusion.8
  86.5 2.6 convolution_add_fusion
  89.2 0.7 copy-done.16
  90.3 1.1 reduce-window.28
  91.4 0.2 slice_reduce_fusion
  92.0 0.2 fusion.17
  92.2 0.2 convolution_reduce_fusion
  92.5 0.7 all_to_all.20
  93.1 3.4 all-to-all-start.1
  96.6 88.4 %all-reduce.3.cloned.1.call-done = f32[256,2304]{1,0:T(8,128)} async-done(((f32[256,2304]{1,0:T(8,128)}), f32[256,2304]{1,0:T(8,128)}) %all-reduce.3.cloned.1.call-update) | async-done | bytes 2359312 | tf_op jit(solution)/shard_map/psum | solution.py:154
  185.0 2.5 multiply_reduce_fusion
  187.7 0.3 copy-done.7
  188.0 0.4 multiply_convert_fusion
  188.5 1.0 copy-done.3
  189.5 0.5 fusion.73
  190.3 0.6 copy.92
  190.9 3.7 %all-to-all-start.2 = ((bf16[8,72,16]{1,2,0:T(8,128)(2,1)}), bf16[8,72,16]{1,2,0:T(8,128)(2,1)S(1)}, u32[]{:S(2)}, u32[]{:S(2)}) async-start(bf16[8,72,16]{1,2,0:T(8,128)(2,1)} %copy.92), calls=%async_computation.2 | async-start | bytes 65536 | tf_op jit(solution)/shard_map/all_to_all | solution.py:200
  194.6 3.7 %convolution_convert_fusion = bf16[576,2304]{1,0:T(8,128)(2,1)} fusion(pred[256,576]{0,1:T(8,128)(4,1)S(1)} %fusion.17, bf16[256,2304]{1,0:T(8,128)(2,1)} %copy-done.3), kind=kOutput, calls=%fused_computation.8 | convolution fusion | flops 680804352 | bytes 3981312 | tf_op jit(solution)/shard_map/ts,td->sd/dot_general | solution.py:194
  198.2 1.2 all-to-all-done.2
  199.4 3.6 all-to-all-start
  203.5 32.1 %all-to-all-done = bf16[8,72,2304]{2,1,0:T(8,128)(2,1)S(1)} async-done(((bf16[8,72,2304]{2,1,0:T(8,128)(2,1)}), bf16[8,72,2304]{2,1,0:T(8,128)(2,1)S(1)}, u32[]{:S(2)}, u32[]{:S(2)}) %all-to-all-start) | async-done | bytes 2654240 | tf_op jit(solution)/shard_map/all_to_all | solution.py:197
  235.6 11.4 %fusion.72 = f32[576,2880]{1,0:T(8,128)S(1)} fusion(bf16[576,2304]{1,0:T(8,128)(2,1)S(1)} %bitcast.153, bf16[2304,2880]{0,1:T(8,128)(2,1)} %bitcast.173), kind=kOutput, calls=%fused_computation.165 | convolution fusion | flops 7644119040 | bytes 22560768 | tf_op jit(solution)/shard_map/dot_general | solution.py:216
  247.0 1.3 multiply_add_fusion
  248.3 9.2 %fusion.5 = bf16[576,2304]{1,0:T(8,128)(2,1)} fusion(bf16[1,1440,2304]{2,1,0:T(8,128)(2,1)} %param.30, f32[576,2880]{1,0:T(8,128)S(1)} %multiply_add_fusion), kind=kOutput, calls=%fused_computation.7 | convolution fusion | flops 3828363264 | bytes 16367616 | tf_op jit(solution)/shard_map/dot_general | solution.py:227
  257.5 4.5 %all-to-all-start.3 = ((bf16[8,72,2304]{2,1,0:T(8,128)(2,1)}), bf16[8,72,2304]{2,1,0:T(8,128)(2,1)}, u32[]{:S(2)}, u32[]{:S(2)}) async-start(bf16[8,72,2304]{2,1,0:T(8,128)(2,1)} %bitcast.152), calls=%async_computation.3 | async-start | bytes 5308416 | tf_op jit(solution)/shard_map/all_to_all | solution.py:230
  262.0 0.3 all-reduce.5.cloned.1.call-start
  262.6 0.4 fusion.71
  263.0 3.6 gather_fusion
  266.9 0.2 select_reduce_fusion
  267.1 27.5 %all-to-all-done.3 = bf16[8,72,2304]{2,1,0:T(8,128)(2,1)} async-done(((bf16[8,72,2304]{2,1,0:T(8,128)(2,1)}), bf16[8,72,2304]{2,1,0:T(8,128)(2,1)}, u32[]{:S(2)}, u32[]{:S(2)}) %all-to-all-start.3) | async-done | bytes 2654240 | tf_op jit(solution)/shard_map/all_to_all | solution.py:230
  294.6 5.9 %convolution_convert_fusion.1 = bf16[256,2304]{1,0:T(8,128)(2,1)} fusion(f32[256,576]{0,1:T(8,128)S(1)} %select_reduce_fusion, bf16[576,2304]{1,0:T(8,128)(2,1)} %bitcast.65), kind=kOutput, calls=%fused_computation.12 | convolution fusion | flops 4077453312 | bytes 4423680 | tf_op jit(solution)/shard_map/dot_general | solution.py:236
  300.5 1.1 slice.135
  301.7 0.7 convolution_convert_fusion.2
  302.5 3.0 reshape.581
  305.5 6.7 %copy.94 = bf16[6,128,2,576]{1,3,2,0:T(8,128)(2,1)} copy(bf16[6,128,2,576]{3,2,1,0:T(2,128)(2,1)} %reshape.581) | data formatting | bytes 3538944
  312.2 41.7 %all-reduce.5.cloned.1.call-done = bf16[256,2304]{1,0:T(8,128)(2,1)} async-done(((bf16[256,2304]{1,0:T(8,128)(2,1)}), bf16[256,2304]{1,0:T(8,128)(2,1)}) %all-reduce.5.cloned.1.call-update) | async-done | bytes 1179664 | tf_op jit(solution)/shard_map/psum | solution.py:237
  353.8 3.7 %add_convert_fusion = bf16[256,2304]{1,0:T(8,128)(2,1)} fusion(bf16[256,2304]{1,0:T(8,128)(2,1)} %all-reduce.5.cloned.1.call-done, f32[256,2304]{1,0:T(8,128)} %all-reduce.3.cloned.1.call-done, bf16[256,2304]{1,0:T(8,128)(2,1)} %param.18), kind=kLoop, calls=%fused_computation.22 | loop fusion | flops 2949120 | bytes 5898240 | tf_op jit(solution)/shard_map/convert_element_type | solution.py:238
  (86 shorter events, 3.4 us)
Async XLA Ops:
  7.2 79.4 %copy-start = (bf16[576,2304]{1,0:T(8,128)(2,1)S(1)}, bf16[576,2304]{1,0:T(8,128)(2,1)}, u32[]{:S(2)}) copy-start(bf16[576,2304]{1,0:T(8,128)(2,1)} %param.27) | copy-start | bytes 7962628
  7.2 44.8 %copy-start.14 = (bf16[2,16,3,576]{3,1,2,0:T(8,128)(2,1)S(1)}, bf16[2,16,3,576]{3,1,2,0:T(8,128)(2,1)}, u32[]{:S(2)}) copy-start(bf16[2,16,3,576]{3,1,2,0:T(8,128)(2,1)} %param.33) | copy-start | bytes 331780
  7.2 57.0 %copy-start.18 = (f32[2304]{0:T(1024)S(1)}, f32[2304]{0:T(1024)}, u32[]{:S(2)}) copy-start(f32[2304]{0:T(1024)} %param.24) | copy-start | bytes 27652
  7.2 63.8 %all-gather.3.cloned.1.call-start = ((), (), s32[]{:S(2)}) async-start(), calls=%async_computation.4 | async-start | bytes 5308416 | tf_op jit(solution)/shard_map/all_gather | solution.py:74
  7.9 76.1 %all-gather.5.cloned.1.call-start = ((), (), s32[]{:S(2)}) async-start(), calls=%async_computation.5 | async-start | bytes 1327104 | tf_op jit(solution)/shard_map/all_gather | solution.py:77
  8.7 176.3 %all-reduce.3.cloned.1.call-start = ((), (), s32[]{:S(2)}) async-start(), calls=%async_computation.6 | async-start | bytes 4718592 | tf_op jit(solution)/shard_map/psum | solution.py:154
  10.4 53.8 %copy-start.5 = (bf16[256,2304]{1,0:T(8,128)(2,1)S(1)}, bf16[256,2304]{1,0:T(8,128)(2,1)}, u32[]{:S(2)}) copy-start(bf16[256,2304]{1,0:T(8,128)(2,1)} %param.18) | copy-start | bytes 3538948
  71.0 1.5 copy-start.6
  71.0 2.5 slice-start
  73.6 1.3 copy-start.9
  73.6 1.8 copy-start.10
  75.9 1.2 copy-start.8
  78.1 3.4 copy-start.12
  89.2 0.7 copy-start.16
  93.1 97.8 %all-to-all-start.1 = ((bf16[8,1,72]{2,1,0:T(2,128)(2,1)}), bf16[8,1,72]{2,1,0:T(2,128)(2,1)S(1)}, u32[]{:S(2)}, u32[]{:S(2)}) async-start(bf16[8,1,72]{2,1,0:T(2,128)(2,1)} %all_to_all.20), calls=%async_computation.1 | async-start | bytes 8192 | tf_op jit(solution)/shard_map/all_to_all | solution.py:203
  96.6 90.9 %copy-start.17 = (f32[2304]{0:T(1024)S(1)}, f32[2304]{0:T(1024)}, u32[]{:S(2)}) copy-start(f32[2304]{0:T(1024)} %param.25) | copy-start | bytes 27652
  185.0 2.7 copy-start.2
  185.0 3.0 copy-start.7
  188.0 1.5 slice-start.1
  188.4 1.0 copy-start.3
  190.9 8.5 %all-to-all-start.2 = ((bf16[8,72,16]{1,2,0:T(8,128)(2,1)}), bf16[8,72,16]{1,2,0:T(8,128)(2,1)S(1)}, u32[]{:S(2)}, u32[]{:S(2)}) async-start(bf16[8,72,16]{1,2,0:T(8,128)(2,1)} %copy.92), calls=%async_computation.2 | async-start | bytes 65536 | tf_op jit(solution)/shard_map/all_to_all | solution.py:200
  199.4 36.2 %all-to-all-start = ((bf16[8,72,2304]{2,1,0:T(8,128)(2,1)}), bf16[8,72,2304]{2,1,0:T(8,128)(2,1)S(1)}, u32[]{:S(2)}, u32[]{:S(2)}) async-start(bf16[8,72,2304]{2,1,0:T(8,128)(2,1)} %bitcast.55), calls=%async_computation | async-start | bytes 5308416 | tf_op jit(solution)/shard_map/all_to_all | solution.py:197
  235.6 11.4 %copy-start.11 = (bf16[1,256,2,1440]{1,3,2,0:T(8,128)(2,1)S(1)}, bf16[1,256,2,1440]{1,3,2,0:T(8,128)(2,1)}, u32[]{:S(2)}) copy-start(bf16[1,256,2,1440]{1,3,2,0:T(8,128)(2,1)} %param.31) | copy-start | bytes 4423684
  257.5 5.1 %copy-start.4 = (bf16[256,2304]{1,0:T(8,128)(2,1)S(1)}, bf16[256,2304]{1,0:T(8,128)(2,1)}, u32[]{:S(2)}) copy-start(bf16[256,2304]{1,0:T(8,128)(2,1)} %copy-done.3) | copy-start | bytes 3538948
  257.5 5.1 %copy-start.15 = (bf16[2304,8]{0,1:T(8,128)(2,1)S(1)}, bf16[2304,8]{0,1:T(8,128)(2,1)}, u32[]{:S(2)}) copy-start(bf16[2304,8]{0,1:T(8,128)(2,1)} %param.28) | copy-start | bytes 110596
  257.5 37.1 %all-to-all-start.3 = ((bf16[8,72,2304]{2,1,0:T(8,128)(2,1)}), bf16[8,72,2304]{2,1,0:T(8,128)(2,1)}, u32[]{:S(2)}, u32[]{:S(2)}) async-start(bf16[8,72,2304]{2,1,0:T(8,128)(2,1)} %bitcast.152), calls=%async_computation.3 | async-start | bytes 5308416 | tf_op jit(solution)/shard_map/all_to_all | solution.py:230
  262.0 91.8 %all-reduce.5.cloned.1.call-start = ((), (), s32[]{:S(2)}) async-start(), calls=%async_computation.7 | async-start | bytes 2359296 | tf_op jit(solution)/shard_map/psum | solution.py:237
  294.6 7.0 %copy-start.13 = (bf16[256,9,32]{0,2,1:T(8,128)(2,1)S(1)}, bf16[256,9,32]{0,2,1:T(8,128)(2,1)}, u32[]{:S(2)}) copy-start(bf16[256,9,32]{0,2,1:T(8,128)(2,1)} %copy-done.12) | copy-start | bytes 442372
  305.5 52.0 %copy-start.1 = (bf16[576,2304]{1,0:T(8,128)(2,1)S(1)}, bf16[576,2304]{1,0:T(8,128)(2,1)}, u32[]{:S(2)}) copy-start(bf16[576,2304]{1,0:T(8,128)(2,1)} %param.27) | copy-start | bytes 7962628
Sparse Core Ops, SparseCore 0:
  9.9 42.8 all-gather.2
  54.7 24.0 all-gather.4
  89.3 95.5 all-reduce.2
  300.6 53.1 all-reduce.4
where the time goes:
time: 365 us; the launch traced here: 364 us
  waiting for transfers between devices  192 us (53%)
  matrix products  52.9 us (14%)
  other arithmetic  35.5 us (10%)
  local copies, waits for them, and re-layouts  29.5 us (8%)
  blocking collectives  24 us (7%)
  starting transfers between devices  15.6 us (4%)
  between operations  14.2 us (4%)
    psum x1, waiting for transfers between devices, per_device(): mixed_out = lax.psum(head_term, 'tp')  88.4 us
    psum x1, waiting for transfers between devices, per_device(): moe_sum = lax.psum(moe_part.astype(jnp.bfloat16), 'tp').astype(jnp.float32)  41.7 us
    all_to_all x1, waiting for transfers between devices, per_device(): lax.all_to_all(spread_copies(send_rows), 'req', split_axis=0, concat_axis...  32.1 us
    all_to_all x1, waiting for transfers between devices, per_device(): lax.all_to_all(partial_term.reshape(n_req, count, D), 'req', split_axis=0...  27.5 us
    gather x3, other arithmetic, per_device(): token_slot = slot_of[adapter]  12.5 us
    unnamed x40, local copies, waits for them, and re-layouts  12.2 us
    all_gather x1, blocking collectives, per_device(): lax.all_gather(pool_aout, 'req', axis=0, tiled=True)  12 us
    all_gather x1, blocking collectives, per_device(): lax.all_gather(slot_query_key_value_up, 'req', axis=0, tiled=True)  12 us
  transfers between devices with their start and end apart: 8, of which 5 were waited for; matrix products, arithmetic and copies ran while one was open for 20% of the time, Pallas kernels for 0%

commit v1 on v0

--- a/solution.py
+++ b/solution.py
@@ -151,7 +151,7 @@
         jnp.dot(attention_result, output_weight, preferred_element_type=jnp.float32)
         + adapter_scale * output_update
     )
-    mixed_out = lax.psum(head_term, "tp")
+    mixed_out = jnp.sum(lax.all_gather(head_term, "tp"), axis=0)
     residual_stream = activations.astype(jnp.float32) + mixed_out
     normed_moe = rms_norm(residual_stream, moe_gain).astype(jnp.bfloat16)
     logits = jnp.dot(normed_moe, router, preferred_element_type=jnp.float32)

time: 365 us -> 440 us (1.21)
  waiting for transfers between devices: 192 us -> 263 us
  other arithmetic: 35.5 us -> 40 us
    all_gather x0 -> x1, waiting for transfers between devices: none -> 159 us  [per_device(): mixed_out = jnp.sum(lax.all_gather(head_term, 'tp'), axis=0)]
    psum x1 -> x0, waiting for transfers between devices: 88.4 us -> none  [per_device(): mixed_out = lax.psum(head_term, 'tp')]
    reduce_sum x0 -> x1, other arithmetic: none -> 4.53 us  [per_device(): mixed_out = jnp.sum(lax.all_gather(head_term, 'tp'), axis=0)]
  transfers between devices with their start and end apart: 8 -> 8, of which waited for: 5 -> 5; matrix products, arithmetic and copies ran while one was open for 20% -> 18% of each run, Pallas kernels for 0% -> 0%
where the time goes in v1:
time: 440 us; the launch traced here: 438 us
  waiting for transfers between devices  263 us (60%)
  matrix products  52.8 us (12%)
  other arithmetic  40 us (9%)
  local copies, waits for them, and re-layouts  29 us (7%)
  blocking collectives  24 us (5%)
  starting transfers between devices  15.7 us (4%)
  between operations  14.3 us (3%)
    all_gather x1, waiting for transfers between devices, per_device(): mixed_out = jnp.sum(lax.all_gather(head_term, 'tp'), axis=0)  159 us
    psum x1, waiting for transfers between devices, per_device(): moe_sum = lax.psum(moe_part.astype(jnp.bfloat16), 'tp').astype(jnp.float32)  40.8 us
    all_to_all x1, waiting for transfers between devices, per_device(): lax.all_to_all(spread_copies(send_rows), 'req', split_axis=0, concat_axis...  32.1 us
    all_to_all x1, waiting for transfers between devices, per_device(): lax.all_to_all(partial_term.reshape(n_req, count, D), 'req', split_axis=0...  27.5 us
    gather x3, other arithmetic, per_device(): token_slot = slot_of[adapter]  12.5 us
    all_gather x1, blocking collectives, per_device(): lax.all_gather(pool_aout, 'req', axis=0, tiled=True)  12.1 us
    all_gather x1, blocking collectives, per_device(): lax.all_gather(slot_query_key_value_up, 'req', axis=0, tiled=True)  11.9 us
    unnamed x40, local copies, waits for them, and re-layouts  11.6 us
  transfers between devices with their start and end apart: 8, of which 5 were waited for; matrix products, arithmetic and copies ran while one was open for 18% of the time, Pallas kernels for 0%

profile of v1, /device:TPU:0, one launch (start us, length us, event | category | flops | bytes accessed | tf_op | source)
XLA Modules:
  0.0 438.3 jit_solution(7538993669030255398)
XLA Ops:
  7.2 0.7 all-gather.5.cloned.1.call-update
  8.0 0.7 all-gather.7.cloned.1.call-update
  8.7 0.7 and_select_fusion.4
  9.4 0.8 reduce-window.27
  10.4 0.8 bitcast_subtract_fusion.2
  11.3 1.6 fusion.10
  12.9 1.4 fusion.63
  14.3 1.6 fusion.66
  15.8 1.9 fusion.62
  17.8 6.8 %compare_select_fusion.9 = (s32[256,1]{0,1:T(1,128)S(1)}, s32[256,1]{0,1:T(1,128)S(1)}, s32[256,1]{0,1:T(1,128)S(1)}) fusion(s32[]{:T(128)} %bitcast.20, s32[]{:T(128)} %bitcast.21, s32[]{:T(128)} %bitcast.22, s32[]{:T(128)} %bitcast.23, s32[]{:T(128)} %bitcast.24, s32[]{:T(128)} %bitcast.26, s32[]{:T(128)} %bitcast.25, s32[]{:T(128)} %bitcast.10, ...), kind=kLoop, calls=%fused_computation.105 | loop fusion | flops 6144 | bytes 4140 | tf_op jit(solution)/shard_map/gather | solution.py:72
  24.7 5.6 %select_select_fusion.2 = s32[256]{0:T(256)S(1)} fusion(pred[256]{0:T(512)(128)(4,1)S(1)} %get-tuple-element.22, pred[256]{0:T(512)(128)(4,1)S(1)} %get-tuple-element.21, pred[256]{0:T(512)(128)(4,1)S(1)} %get-tuple-element.20, pred[256]{0:T(512)(128)(4,1)S(1)} %get-tuple-element.19, pred[256]{0:T(512)(128)(4,1)S(1)} %get-tuple-element.18, ...), kind=kLoop, calls=%fused_computation.137 | loop fusion | flops 2304 | bytes 4388 | tf_op jit(solution)/shard_map/gather | solution.py:72
  30.3 0.7 fusion.64
  31.0 8.8 %fusion.49 = (s32[256,1]{0,1:T(1,128)S(1)}, s32[256,1]{0,1:T(1,128)S(1)}) fusion(s32[]{:T(128)} %bitcast.72, s32[]{:T(128)} %bitcast.73, s32[]{:T(128)} %bitcast.74, s32[]{:T(128)} %bitcast.68, s32[]{:T(128)} %bitcast.75, s32[]{:T(128)} %bitcast.69, s32[]{:T(128)} %bitcast.77, s32[]{:T(128)} %bitcast.76, s32[]{:T(128)} %bitcast.71, s32[]{:T(128)} %bitcast.70, ...), kind=kLoop, calls=%fused_computation.132 | loop fusion | flops 11008 | bytes 3128 | tf_op jit(solution)/shard_map/mul | solution.py:112
  39.9 12.1 %all_gather.20 = bf16[16,576,16]{1,2,0:T(8,128)(2,1)S(1)} all-gather(bf16[2,576,16]{1,2,0:T(8,128)(2,1)} %param.34), channel_id=1, replica_groups=mesh['req'=8,'tp'=4] {'req'}, dimensions={0}, use_global_device_ids=true | all-gather | bytes 331776 | tf_op jit(solution)/shard_map/all_gather | solution.py:76
  52.0 11.9 %all_gather.19 = bf16[16,16,3,576]{3,1,2,0:T(8,128)(2,1)} all-gather(bf16[2,16,3,576]{3,1,2,0:T(8,128)(2,1)S(1)} %copy-done.14), channel_id=1, replica_groups=mesh['req'=8,'tp'=4] {'req'}, dimensions={0}, use_global_device_ids=true | all-gather | bytes 995328 | tf_op jit(solution)/shard_map/all_gather | solution.py:75
  63.9 0.2 multiply_cosine_fusion
  64.1 6.8 %fusion.1 = f32[256,3,576]{0,2,1:T(8,128)} fusion(bf16[2304,3,576]{0,2,1:T(8,128)(2,1)} %param.26, bf16[256,2304]{1,0:T(8,128)(2,1)S(1)} %copy-done.5, f32[2304]{0:T(1024)S(1)} %copy-done.18, f32[256]{0:T(256)S(1)} %add_rsqrt_fusion.1), kind=kOutput, calls=%fused_computation.2 | convolution fusion | flops 2040791040 | bytes 10921984 | tf_op jit(solution)/shard_map/dot_general | solution.py:99
  71.0 1.4 copy-done.6
  72.4 1.2 slice-done
  73.5 1.2 fusion.25
  74.8 0.5 copy-done.10
  75.3 0.5 bitcast_add_fusion
  75.8 1.2 copy-done.8
  77.1 0.8 subtract_convert_fusion
  78.0 3.4 fusion.67
  81.4 2.2 convolution_convert_fusion.3
  83.6 0.3 fusion.74
  83.9 2.5 fusion.8
  86.4 2.5 convolution_add_fusion
  89.0 0.7 copy-done.16
  90.1 1.1 reduce-window.28
  91.2 0.2 slice_reduce_fusion
  91.8 0.2 fusion.17
  92.0 0.2 convolution_reduce_fusion
  92.3 0.7 all_to_all.20
  92.9 3.5 all-to-all-start.1
  96.5 159.5 %all-gather.9.cloned.1.call-done = f32[1024,2304]{1,0:T(8,128)} async-done(((f32[256,2304]{1,0:T(8,128)}), f32[1024,2304]{1,0:T(8,128)}) %all-gather.9.cloned.1.call-update) | async-done | bytes 9437200 | tf_op jit(solution)/shard_map/all_gather | solution.py:154
  255.9 4.5 %reduce_sum.104 = f32[256,2304]{1,0:T(8,128)S(1)} reduce(f32[4,256,2304]{2,1,0:T(8,128)} %bitcast.148, f32[]{:T(128)} %constant.84.clone.1), dimensions={0}, to_apply=%region_7.8 | reduce | flops 1769472 | bytes 11796484 | tf_op jit(solution)/shard_map/reduce_sum | solution.py:154
  260.5 2.5 multiply_reduce_fusion
  263.1 0.4 multiply_convert_fusion
  263.5 1.0 copy-done.3
  264.5 0.5 fusion.73
  265.4 0.6 copy.92
  266.0 3.7 all-to-all-start.2
  269.7 3.7 convolution_convert_fusion
  273.3 1.2 all-to-all-done.2
  274.5 3.6 all-to-all-start
  278.6 32.1 %all-to-all-done = bf16[8,72,2304]{2,1,0:T(8,128)(2,1)S(1)} async-done(((bf16[8,72,2304]{2,1,0:T(8,128)(2,1)}), bf16[8,72,2304]{2,1,0:T(8,128)(2,1)S(1)}, u32[]{:S(2)}, u32[]{:S(2)}) %all-to-all-start) | async-done | bytes 2654240 | tf_op jit(solution)/shard_map/all_to_all | solution.py:197
  310.7 11.4 %fusion.72 = f32[576,2880]{1,0:T(8,128)S(1)} fusion(bf16[576,2304]{1,0:T(8,128)(2,1)S(1)} %bitcast.155, bf16[2304,2880]{0,1:T(8,128)(2,1)} %bitcast.175), kind=kOutput, calls=%fused_computation.165 | convolution fusion | flops 7644119040 | bytes 22560768 | tf_op jit(solution)/shard_map/dot_general | solution.py:216
  322.1 1.3 multiply_add_fusion
  323.4 9.2 %fusion.5 = bf16[576,2304]{1,0:T(8,128)(2,1)} fusion(bf16[1,1440,2304]{2,1,0:T(8,128)(2,1)} %param.30, f32[576,2880]{1,0:T(8,128)S(1)} %multiply_add_fusion), kind=kOutput, calls=%fused_computation.7 | convolution fusion | flops 3828363264 | bytes 16367616 | tf_op jit(solution)/shard_map/dot_general | solution.py:227
  332.6 4.5 %all-to-all-start.3 = ((bf16[8,72,2304]{2,1,0:T(8,128)(2,1)}), bf16[8,72,2304]{2,1,0:T(8,128)(2,1)}, u32[]{:S(2)}, u32[]{:S(2)}) async-start(bf16[8,72,2304]{2,1,0:T(8,128)(2,1)} %bitcast.154), calls=%async_computation.3 | async-start | bytes 5308416 | tf_op jit(solution)/shard_map/all_to_all | solution.py:230
  337.1 0.3 all-reduce.2.cloned.1.call-start
  337.7 0.4 fusion.71
  338.1 3.6 gather_fusion
  342.0 0.2 select_reduce_fusion
  342.2 27.5 %all-to-all-done.3 = bf16[8,72,2304]{2,1,0:T(8,128)(2,1)} async-done(((bf16[8,72,2304]{2,1,0:T(8,128)(2,1)}), bf16[8,72,2304]{2,1,0:T(8,128)(2,1)}, u32[]{:S(2)}, u32[]{:S(2)}) %all-to-all-start.3) | async-done | bytes 2654240 | tf_op jit(solution)/shard_map/all_to_all | solution.py:230
  369.7 5.8 %convolution_convert_fusion.1 = bf16[256,2304]{1,0:T(8,128)(2,1)} fusion(f32[256,576]{0,1:T(8,128)S(1)} %select_reduce_fusion, bf16[576,2304]{1,0:T(8,128)(2,1)} %bitcast.66), kind=kOutput, calls=%fused_computation.12 | convolution fusion | flops 4077453312 | bytes 4423680 | tf_op jit(solution)/shard_map/dot_general | solution.py:236
  375.6 1.1 slice.135
  376.8 0.7 convolution_convert_fusion.2
  377.5 3.0 reshape.581
  380.5 6.7 %copy.94 = bf16[6,128,2,576]{1,3,2,0:T(8,128)(2,1)} copy(bf16[6,128,2,576]{3,2,1,0:T(2,128)(2,1)} %reshape.581) | data formatting | bytes 3538944
  387.2 40.8 %all-reduce.2.cloned.1.call-done = bf16[256,2304]{1,0:T(8,128)(2,1)} async-done(((bf16[256,2304]{1,0:T(8,128)(2,1)}), bf16[256,2304]{1,0:T(8,128)(2,1)}) %all-reduce.2.cloned.1.call-update) | async-done | bytes 1179664 | tf_op jit(solution)/shard_map/psum | solution.py:237
  428.0 3.7 add_convert_fusion
  (87 shorter events, 3.2 us)
Async XLA Ops:
  7.2 79.3 %copy-start = (bf16[576,2304]{1,0:T(8,128)(2,1)S(1)}, bf16[576,2304]{1,0:T(8,128)(2,1)}, u32[]{:S(2)}) copy-start(bf16[576,2304]{1,0:T(8,128)(2,1)} %param.27) | copy-start | bytes 7962628
  7.2 44.8 %copy-start.14 = (bf16[2,16,3,576]{3,1,2,0:T(8,128)(2,1)S(1)}, bf16[2,16,3,576]{3,1,2,0:T(8,128)(2,1)}, u32[]{:S(2)}) copy-start(bf16[2,16,3,576]{3,1,2,0:T(8,128)(2,1)} %param.33) | copy-start | bytes 331780
  7.2 56.9 %copy-start.18 = (f32[2304]{0:T(1024)S(1)}, f32[2304]{0:T(1024)}, u32[]{:S(2)}) copy-start(f32[2304]{0:T(1024)} %param.24) | copy-start | bytes 27652
  7.2 63.8 %all-gather.5.cloned.1.call-start = ((), (), s32[]{:S(2)}) async-start(), calls=%async_computation.4 | async-start | bytes 5308416 | tf_op jit(solution)/shard_map/all_gather | solution.py:74
  7.9 76.0 %all-gather.7.cloned.1.call-start = ((), (), s32[]{:S(2)}) async-start(), calls=%async_computation.5 | async-start | bytes 1327104 | tf_op jit(solution)/shard_map/all_gather | solution.py:77
  8.7 247.2 %all-gather.9.cloned.1.call-start = ((), (), s32[]{:S(2)}) async-start(), calls=%async_computation.7 | async-start | bytes 11796480 | tf_op jit(solution)/shard_map/all_gather | solution.py:154
  10.4 53.7 %copy-start.5 = (bf16[256,2304]{1,0:T(8,128)(2,1)S(1)}, bf16[256,2304]{1,0:T(8,128)(2,1)}, u32[]{:S(2)}) copy-start(bf16[256,2304]{1,0:T(8,128)(2,1)} %param.18) | copy-start | bytes 3538948
  71.0 1.4 copy-start.6
  71.0 2.5 slice-start
  73.5 1.3 copy-start.9
  73.5 1.8 copy-start.10
  75.8 1.2 copy-start.8
  78.0 3.4 copy-start.12
  89.0 0.7 copy-start.16
  92.9 173.0 %all-to-all-start.1 = ((bf16[8,1,72]{2,1,0:T(2,128)(2,1)}), bf16[8,1,72]{2,1,0:T(2,128)(2,1)S(1)}, u32[]{:S(2)}, u32[]{:S(2)}) async-start(bf16[8,1,72]{2,1,0:T(2,128)(2,1)} %all_to_all.20), calls=%async_computation.1 | async-start | bytes 8192 | tf_op jit(solution)/shard_map/all_to_all | solution.py:203
  260.5 3.0 copy-start.2
  260.5 2.6 copy-start.7
  260.5 2.6 copy-start.17
  263.0 1.5 slice-start.1
  263.5 1.0 copy-start.3
  266.0 8.5 %all-to-all-start.2 = ((bf16[8,72,16]{1,2,0:T(8,128)(2,1)}), bf16[8,72,16]{1,2,0:T(8,128)(2,1)S(1)}, u32[]{:S(2)}, u32[]{:S(2)}) async-start(bf16[8,72,16]{1,2,0:T(8,128)(2,1)} %copy.92), calls=%async_computation.2 | async-start | bytes 65536 | tf_op jit(solution)/shard_map/all_to_all | solution.py:200
  274.5 36.2 %all-to-all-start = ((bf16[8,72,2304]{2,1,0:T(8,128)(2,1)}), bf16[8,72,2304]{2,1,0:T(8,128)(2,1)S(1)}, u32[]{:S(2)}, u32[]{:S(2)}) async-start(bf16[8,72,2304]{2,1,0:T(8,128)(2,1)} %bitcast.56), calls=%async_computation | async-start | bytes 5308416 | tf_op jit(solution)/shard_map/all_to_all | solution.py:197
  310.7 11.4 %copy-start.11 = (bf16[1,256,2,1440]{1,3,2,0:T(8,128)(2,1)S(1)}, bf16[1,256,2,1440]{1,3,2,0:T(8,128)(2,1)}, u32[]{:S(2)}) copy-start(bf16[1,256,2,1440]{1,3,2,0:T(8,128)(2,1)} %param.31) | copy-start | bytes 4423684
  332.6 5.1 %copy-start.4 = (bf16[256,2304]{1,0:T(8,128)(2,1)S(1)}, bf16[256,2304]{1,0:T(8,128)(2,1)}, u32[]{:S(2)}) copy-start(bf16[256,2304]{1,0:T(8,128)(2,1)} %copy-done.3) | copy-start | bytes 3538948
  332.6 5.1 %copy-start.15 = (bf16[2304,8]{0,1:T(8,128)(2,1)S(1)}, bf16[2304,8]{0,1:T(8,128)(2,1)}, u32[]{:S(2)}) copy-start(bf16[2304,8]{0,1:T(8,128)(2,1)} %param.28) | copy-start | bytes 110596
  332.6 37.1 %all-to-all-start.3 = ((bf16[8,72,2304]{2,1,0:T(8,128)(2,1)}), bf16[8,72,2304]{2,1,0:T(8,128)(2,1)}, u32[]{:S(2)}, u32[]{:S(2)}) async-start(bf16[8,72,2304]{2,1,0:T(8,128)(2,1)} %bitcast.154), calls=%async_computation.3 | async-start | bytes 5308416 | tf_op jit(solution)/shard_map/all_to_all | solution.py:230
  337.1 90.9 %all-reduce.2.cloned.1.call-start = ((), (), s32[]{:S(2)}) async-start(), calls=%async_computation.6 | async-start | bytes 2359296 | tf_op jit(solution)/shard_map/psum | solution.py:237
  369.7 7.0 %copy-start.13 = (bf16[256,9,32]{0,2,1:T(8,128)(2,1)S(1)}, bf16[256,9,32]{0,2,1:T(8,128)(2,1)}, u32[]{:S(2)}) copy-start(bf16[256,9,32]{0,2,1:T(8,128)(2,1)} %copy-done.12) | copy-start | bytes 442372
  380.5 51.2 %copy-start.1 = (bf16[576,2304]{1,0:T(8,128)(2,1)S(1)}, bf16[576,2304]{1,0:T(8,128)(2,1)}, u32[]{:S(2)}) copy-start(bf16[576,2304]{1,0:T(8,128)(2,1)} %param.27) | copy-start | bytes 7962628
Sparse Core Ops, SparseCore 0:
  9.9 42.8 all-gather.4
  54.7 24.0 all-gather.6
  89.1 166.7 all-gather.8
  375.7 52.2 all-reduce.1
